TPU v7x, 32 devices: a whole 2x2x4 slice. The times are simulated.
32 devices in a mesh: ctx: 8 (over z, x), head: 4 (over y, core).
Axes of the slice: x: 2, y: 2, z: 4, core: 2. Of those that a mesh axis runs over, the one named last changes fastest.
Arguments:
- queries: bfloat16 [2048, 32, 128], P('ctx', 'head'), may hold values from -40 to 40
- keys: bfloat16 [2048, 8, 128], P('ctx', 'head'), may hold values from -40 to 40
- values: bfloat16 [2048, 8, 128], P('ctx', 'head'), may hold values from -6 to 6
- doc_ids: int32 [2048], P('ctx'), may hold values from 0 to 3, never falling along the last dimension, each value on 1 to 1024 neighbouring positions
Outputs:
- attended: bfloat16 [2048, 4096], P(('ctx', 'head'))
Inputs may be any that keep to these rules, and one draw needn't show every extreme that they name: `doc_ids`: document numbers never fall along the sequence; each document has 1 to 1024 tokens and one has exactly 1024.
All inputs are finite; a program needn't handle non-finite values.
Results may differ from a plain program's by a relative error of at most 0.009.
Values may be sent and summed in bfloat16 or wider, within the bound.
A program may use at most 128 MiB of HBM per device.

v0:
```python
import jax
import jax.numpy as jnp
from jax import lax
from jax.sharding import PartitionSpec as P


def shifted(shard, axis, by):
    devices = lax.axis_size(axis)
    return lax.ppermute(shard, axis, [(i, (i + by) % devices) for i in range(devices)])


def attend(query_sets, keys, values, all_ids):
    kv_heads = keys.shape[1]
    head_dim = keys.shape[2]
    score_scale = head_dim ** (-0.5)
    prepared = []
    initial = []
    for query_rows, query_start in query_sets:
        row_count = query_rows.shape[0]
        q_heads = query_rows.shape[1]
        group_size = q_heads // kv_heads
        grouped = query_rows.reshape(row_count, kv_heads, group_size, head_dim)
        query_pos = query_start + jnp.arange(row_count, dtype=jnp.int32)
        query_ids = lax.dynamic_slice_in_dim(all_ids, query_start, row_count, 0)
        last_pos = query_start + row_count - 1
        prepared.append((grouped, query_pos, query_ids, last_pos))
        initial.append(
            (
                jnp.full((kv_heads, group_size, row_count), -1e30, jnp.float32),
                jnp.zeros((kv_heads, group_size, row_count), jnp.float32),
                jnp.zeros((kv_heads, group_size, row_count, head_dim), jnp.float32),
            )
        )
    carried = tuple(initial)
    key_start = jnp.int32(0)
    key_piece = lax.all_gather(keys, "ctx", axis=0, tiled=True)
    value_piece = lax.all_gather(values, "ctx", axis=0, tiled=True)
    piece_len = key_piece.shape[0]
    key_pos = jnp.arange(piece_len, dtype=jnp.int32)
    updated = []
    for (grouped, query_pos, query_ids, last_pos), state_now in zip(prepared, carried):

        def update(state_old, grouped=grouped, query_pos=query_pos, query_ids=query_ids):
            old_max, old_sum, accumulated = state_old
            scores = (
                jnp.einsum("nhgd,khd->hgnk", grouped, key_piece, preferred_element_type=jnp.float32)
                * score_scale
            )
            visible = (key_pos[None, :] <= query_pos[:, None]) & (
                all_ids[None, :] == query_ids[:, None]
            )
            scores = jnp.where(visible, scores, jnp.float32(-1e30))
            new_max = jnp.maximum(old_max, jnp.max(scores, axis=-1))
            weights = jnp.where(visible, jnp.exp(scores - new_max[..., None]), jnp.float32(0.0))
            new_sum = jnp.sum(weights, axis=-1)
            product = jnp.einsum(
                "hgnk,khd->hgnd",
                weights.astype(jnp.bfloat16),
                value_piece,
                preferred_element_type=jnp.float32,
            )
            return (new_max, new_sum, product)

        def unchanged(state_old):
            return state_old

        updated.append(lax.cond(key_start <= last_pos, update, unchanged, state_now))
    finals = tuple(updated)
    outputs = []
    for final_state in finals:
        run_max, run_sum, accumulated = final_state
        normed = accumulated / run_sum[..., None]
        row_count = normed.shape[2]
        joined = jnp.transpose(normed, (2, 0, 1, 3)).reshape(row_count, -1)
        outputs.append(joined.astype(jnp.bfloat16))
    return outputs


def local(queries, keys, values, doc_ids):
    tok_rows = queries.shape[0]
    half_rows = tok_rows // 2
    ctx_count = lax.axis_size("ctx")
    ctx_place = lax.axis_index("ctx")
    all_ids = lax.all_gather(doc_ids, "ctx", axis=0, tiled=True)
    half_axis = ctx_count // 2
    moved_half = shifted(queries[half_rows:], "ctx", half_axis)
    partner = (ctx_place + ctx_count - half_axis) % ctx_count
    query_sets = [
        (queries[:half_rows], ctx_place * tok_rows),
        (moved_half, partner * tok_rows + half_rows),
    ]
    results = attend(query_sets, keys, values, all_ids)
    returned = shifted(results[1], "ctx", half_axis)
    merged = jnp.concatenate([results[0], returned], axis=0)
    return lax.all_to_all(merged, "head", split_axis=0, concat_axis=1, tiled=True)


def solution(mesh):
    return jax.shard_map(
        local,
        mesh=mesh,
        in_specs=(P("ctx", "head", None), P("ctx", "head", None), P("ctx", "head", None), P("ctx")),
        out_specs=P(("ctx", "head"), None),
        check_vma=False,
    )
```

profile of v0, /device:TPU:0, one launch (start us, length us, event | category | flops | bytes accessed | tf_op | source)
XLA Modules:
  0.0 137.6 jit_solution(7778220357033783321)
XLA Ops:
  6.5 0.0 all-gather.4.cloned.1.call-start
  6.5 1.6 %copy.32 = bf16[256,2,128]{2,0,1:T(8,128)(2,1)} copy(bf16[256,2,128]{2,1,0:T(2,128)(2,1)} %param.9) | data formatting | bytes 262144 | tf_op args[1]
  8.1 0.0 all-gather.4.cloned.1.call-update
  8.1 0.0 all-gather.6.cloned.1.call-start
  8.2 1.6 %copy.33 = bf16[256,2,128]{2,0,1:T(8,128)(2,1)} copy(bf16[256,2,128]{2,1,0:T(2,128)(2,1)} %param.10) | data formatting | bytes 262144 | tf_op args[2]
  9.8 0.0 all-gather.6.cloned.1.call-update
  9.8 1.0 slice.8
  10.8 4.1 %collective-permute-start = (bf16[128,8,128]{2,0,1:T(8,128)(2,1)S(1)}, bf16[128,8,128]{2,0,1:T(8,128)(2,1)S(1)}, u32[]{:S(2)}, u32[]{:S(2)}) collective-permute-start(bf16[128,8,128]{2,0,1:T(8,128)(2,1)S(1)} %copy.50), channel_id=1, source_target_pairs={{0,16},{4,20},{8,24},{12,28},{16,0},{20,4},{24,8},{28,12},{1,17},{... | collective-permute-start | bytes 786440 | tf_op jit(solution)/shard_map/ppermute | solution.py:9
  14.9 20.3 %all-gather = s32[8,1,256]{2,1,0:T(1,128)S(1)} all-gather(s32[1,1,256]{2,1,0:T(1,128)} %bitcast.69), channel_id=1, replica_groups=mesh['ctx'=8,'head'=4] {'ctx'}, dimensions={0}, use_global_device_ids=true | all-gather | bytes 9216 | tf_op jit(solution)/shard_map/all_gather | solution.py:84
  35.2 0.0 collective-permute-done
  35.2 19.7 %all-gather.4.cloned.1.call-done = bf16[2048,2,128]{2,0,1:T(8,128)(2,1)} async-done(((bf16[256,2,128]{2,0,1:T(8,128)(2,1)}), bf16[2048,2,128]{2,0,1:T(8,128)(2,1)}) %all-gather.4.cloned.1.call-update) | async-done | bytes 1048592 | tf_op jit(solution)/shard_map/all_gather | solution.py:36
  54.8 41.2 %all-gather.6.cloned.1.call-done = bf16[2048,2,128]{2,0,1:T(8,128)(2,1)} async-done(((bf16[256,2,128]{2,0,1:T(8,128)(2,1)}), bf16[2048,2,128]{2,0,1:T(8,128)(2,1)}) %all-gather.6.cloned.1.call-update) | async-done | bytes 1048592 | tf_op jit(solution)/shard_map/all_gather | solution.py:37
  96.0 0.0 copy-start
  96.0 8.5 %conditional.3 = (f32[2,4,128]{2,1,0:T(4,128)S(1)}, f32[2,4,128,128]{2,3,1,0:T(8,128)S(1)}) conditional(s32[]{:T(128)} %convert_element_type.37, () %tuple.32, (s32[2048]{0:T(1024)S(1)}, s32[]{:T(128)}, s32[128]{0:T(128)S(1)}, s32[2048]{0:T(1024)S(1)}, bf16[128,8,128]{2,0,1:T(8,128)(2,1)S(1)}, /*index=5*/bf16[2048,2,128]{2,0,1:T(8,128)(2,1)}, ...), branch_computations={%region_4.5_spmd, %region_5.8_spmd} | conditional | flops 1101790336 | bytes 33336418 | solution.py:67
  96.0 0.0 copy-start.1
  96.0 0.1 dynamic_slice.10
  96.1 1.3 compare_and_fusion.1
  97.4 2.6 %fusion.12 = (f32[2,4,128]{2,1,0:T(4,128)S(1)}, f32[2,2048,128,4]{2,1,3,0:T(8,128)S(1)}) fusion(pred[128,2048]{0,1:T(8,128)(4,1)S(1)} %compare_and_fusion.1, bf16[128,2,4,128]{3,0,2,1:T(8,128)(2,1)S(1)} %bitcast.70, bf16[2048,2,128]{2,0,1:T(8,128)(2,1)} %get-tuple-element.139), kind=kOutput, calls=%fused_computation.18 | convolution fusion | flops 543161344 | bytes 9965568 | tf_op jit(solution)/shard_map/cond/branch_1_fun/nhgd,khd->hgnk/dot_general | solution.py:46
  100.0 0.0 copy-done.1
  100.0 2.5 %fusion.15 = f32[2,4,128,128]{2,3,1,0:T(8,128)S(1)} fusion(f32[2,2048,128,4]{2,1,3,0:T(8,128)S(1)} %get-tuple-element.183, f32[2,4,128]{2,1,0:T(4,128)S(1)} %broadcast_maximum_fusion.1, pred[128,2048]{0,1:T(8,128)(4,1)S(1)} %compare_and_fusion.1, bf16[2048,2,128]{2,0,1:T(8,128)(2,1)S(1)} %copy-done.1), kind=kOutput, calls=%fused_computation.21 | convolution fusion | flops 547356672 | bytes 10227712 | tf_op jit(solution)/shard_map/cond | solution.py:67
  102.5 2.0 %fusion.14 = f32[2,4,128]{2,1,0:T(4,128)S(1)} fusion(f32[2,2048,128,4]{2,1,3,0:T(8,128)S(1)} %get-tuple-element.183, f32[2,4,128]{2,1,0:T(4,128)S(1)} %broadcast_maximum_fusion.1, pred[128,2048]{0,1:T(8,128)(4,1)S(1)} %compare_and_fusion.1), kind=kLoop, calls=%fused_computation.20 | loop fusion | flops 10484736 | bytes 8658944 | tf_op jit(solution)/shard_map/cond/branch_1_fun/reduce_sum | solution.py:55
  104.6 0.1 divide_convert_fusion
  104.6 0.7 collective-permute-start.1
  105.4 0.0 copy-done
  105.4 8.7 %conditional.2 = (f32[2,4,128]{2,1,0:T(4,128)S(1)}, f32[2,4,128,128]{2,3,1,0:T(8,128)S(1)}) conditional(s32[]{:T(128)} %convert_element_type.33, () %tuple.30, (s32[2048]{0:T(1024)S(1)}, s32[]{:T(128)}, s32[128]{0:T(128)S(1)}, s32[2048]{0:T(1024)S(1)}, bf16[256,8,128]{2,1,0:T(8,128)(2,1)S(1)}, /*index=5*/bf16[2048,2,128]{2,0,1:T(8,128)(2,1)}, ...), branch_computations={%region_0.1_spmd, %region_1.4_spmd} | conditional | flops 1101790336 | bytes 34909272 | solution.py:67
  105.4 0.1 dynamic_slice.9
  105.5 1.3 compare_and_fusion
  106.8 0.0 copy-start.2
  106.8 0.1 copy.34
  106.9 2.7 %fusion = (f32[2,4,128]{2,1,0:T(4,128)S(1)}, f32[2,2048,128,4]{2,1,3,0:T(8,128)S(1)}) fusion(pred[128,2048]{0,1:T(8,128)(4,1)S(1)} %compare_and_fusion, bf16[128,2,4,128]{3,0,2,1:T(8,128)(2,1)S(1)} %bitcast.66, bf16[2048,2,128]{2,0,1:T(8,128)(2,1)} %get-tuple-element.132), kind=kOutput, calls=%fused_computation.2 | convolution fusion | flops 543161344 | bytes 9965568 | tf_op jit(solution)/shard_map/cond/branch_1_fun/nhgd,khd->hgnk/dot_general | solution.py:46
  109.6 0.0 copy-done.2
  109.6 2.5 %fusion.3 = f32[2,4,128,128]{2,3,1,0:T(8,128)S(1)} fusion(f32[2,2048,128,4]{2,1,3,0:T(8,128)S(1)} %get-tuple-element.181, f32[2,4,128]{2,1,0:T(4,128)S(1)} %broadcast_maximum_fusion, pred[128,2048]{0,1:T(8,128)(4,1)S(1)} %compare_and_fusion, bf16[2048,2,128]{2,0,1:T(8,128)(2,1)S(1)} %copy-done.2), kind=kOutput, calls=%fused_computation.5 | convolution fusion | flops 547356672 | bytes 10227712 | tf_op jit(solution)/shard_map/cond | solution.py:67
  112.1 2.0 %fusion.2 = f32[2,4,128]{2,1,0:T(4,128)S(1)} fusion(f32[2,2048,128,4]{2,1,3,0:T(8,128)S(1)} %get-tuple-element.181, f32[2,4,128]{2,1,0:T(4,128)S(1)} %broadcast_maximum_fusion, pred[128,2048]{0,1:T(8,128)(4,1)S(1)} %compare_and_fusion), kind=kLoop, calls=%fused_computation.4 | loop fusion | flops 10484736 | bytes 8658944 | tf_op jit(solution)/shard_map/cond/branch_1_fun/reduce_sum | solution.py:55
  114.1 0.1 divide_convert_fusion.1
  114.2 4.1 %collective-permute-done.1 = bf16[128,1024]{0,1:T(8,128)(2,1)S(1)} collective-permute-done((bf16[128,1024]{0,1:T(8,128)(2,1)S(1)}, bf16[128,1024]{0,1:T(8,128)(2,1)S(1)}, u32[]{:S(2)}, u32[]{:S(2)}) %collective-permute-start.1) | collective-permute-done | bytes 262176 | tf_op jit(solution)/shard_map/ppermute | solution.py:9
  118.3 0.1 pad_maximum_fusion
  118.3 0.2 copy.38
  118.5 11.4 %all_to_all.19 = bf16[4,64,1024]{2,1,0:T(8,128)(2,1)S(1)} all-to-all(bf16[4,64,1024]{2,1,0:T(8,128)(2,1)S(1)} %bitcast.62), channel_id=1, replica_groups=mesh['ctx'=8,'head'=4] {'head'}, dimensions={0} | all-to-all | bytes 1048576 | tf_op jit(solution)/shard_map/all_to_all | solution.py:95
  129.9 0.8 copy.51
  (10 shorter events, 0.1 us)
Async XLA Ops:
  6.5 48.3 %all-gather.4.cloned.1.call-start = ((), (), s32[]{:S(2)}) async-start(), calls=%async_computation.1 | async-start | bytes 1179648 | tf_op jit(solution)/shard_map/all_gather | solution.py:36
  8.1 87.9 %all-gather.6.cloned.1.call-start = ((), (), s32[]{:S(2)}) async-start(), calls=%async_computation.2 | async-start | bytes 1179648 | tf_op jit(solution)/shard_map/all_gather | solution.py:37
  10.8 24.4 %collective-permute-start = (bf16[128,8,128]{2,0,1:T(8,128)(2,1)S(1)}, bf16[128,8,128]{2,0,1:T(8,128)(2,1)S(1)}, u32[]{:S(2)}, u32[]{:S(2)}) collective-permute-start(bf16[128,8,128]{2,0,1:T(8,128)(2,1)S(1)} %copy.50), channel_id=1, source_target_pairs={{0,16},{4,20},{8,24},{12,28},{16,0},{20,4},{24,8},{28,12},{1,17},{... | collective-permute-start | bytes 786440 | tf_op jit(solution)/shard_map/ppermute | solution.py:9
  96.0 9.4 %copy-start = (bf16[256,8,128]{2,1,0:T(8,128)(2,1)S(1)}, bf16[256,8,128]{2,1,0:T(8,128)(2,1)}, u32[]{:S(2)}) copy-start(bf16[256,8,128]{2,1,0:T(8,128)(2,1)} %param.8) | copy-start | bytes 1572868
  96.0 4.0 %copy-start.1 = (bf16[2048,2,128]{2,0,1:T(8,128)(2,1)S(1)}, bf16[2048,2,128]{2,0,1:T(8,128)(2,1)}, u32[]{:S(2)}) copy-start(bf16[2048,2,128]{2,0,1:T(8,128)(2,1)} %get-tuple-element.141) | copy-start | bytes 3145732 | tf_op jit(solution)/shard_map/cond
  104.6 13.6 %collective-permute-start.1 = (bf16[128,1024]{0,1:T(8,128)(2,1)S(1)}, bf16[128,1024]{0,1:T(8,128)(2,1)S(1)}, u32[]{:S(2)}, u32[]{:S(2)}) collective-permute-start(bf16[128,1024]{0,1:T(8,128)(2,1)S(1)} %bitcast.65), channel_id=1, source_target_pairs={{0,16},{4,20},{8,24},{12,28},{16,0},{20,4},{24,8},{28,12},{1,17},{... | collective-permute-start | bytes 786440 | tf_op jit(solution)/shard_map/ppermute | solution.py:9
  106.8 2.8 %copy-start.2 = (bf16[2048,2,128]{2,0,1:T(8,128)(2,1)S(1)}, bf16[2048,2,128]{2,0,1:T(8,128)(2,1)}, u32[]{:S(2)}) copy-start(bf16[2048,2,128]{2,0,1:T(8,128)(2,1)} %get-tuple-element.134) | copy-start | bytes 3145732 | tf_op jit(solution)/shard_map/cond
Sparse Core Ops, SparseCore 0:
  9.5 45.2 all-gather.3
  57.0 38.9 all-gather.5
where the time goes:
time: 138 us
  waiting for transfers between devices  65 us (47%)
  blocking collectives  31.7 us (23%)
  between operations  13.5 us (10%)
  matrix products  10.2 us (7%)
  other arithmetic  6.81 us (5%)
  local copies, waits for them, and re-layouts  5.47 us (4%)
  starting transfers between devices  4.89 us (4%)
    all_gather x1, waiting for transfers between devices, attend(): value_piece = lax.all_gather(values, 'ctx', axis=0, tiled=True)  41.2 us
    all_gather x1, blocking collectives, local(): all_ids = lax.all_gather(doc_ids, 'ctx', axis=0, tiled=True)  20.3 us
    all_gather x1, waiting for transfers between devices, attend(): key_piece = lax.all_gather(keys, 'ctx', axis=0, tiled=True)  19.7 us
    all_to_all x1, blocking collectives, local(): lax.all_to_all(merged, 'head', split_axis=0, concat_axis=1, tiled=True)  11.4 us
    dot_general x2, matrix products, update(): jnp.einsum('nhgd,khd->hgnk', grouped, key_piece, preferred_element_type=j...  5.26 us
    cond x2, matrix products, attend(): lax.cond(key_start <= last_pos, update, unchanged, state_now)  4.99 us
    ppermute x2, starting transfers between devices, shifted(): lax.ppermute(shard, axis, [(i, (i + by) % devices) for i in range(devices)])  4.85 us
    ppermute x2, waiting for transfers between devices, shifted(): lax.ppermute(shard, axis, [(i, (i + by) % devices) for i in range(devices)])  4.11 us
  transfers between devices with their start and end apart: 4, of which 3 were waited for; matrix products, arithmetic and copies ran while one was open for 8% of the time, Pallas kernels for 0%

commit v1 on v0

v1 whole, which is shorter than its diff:
```python
import functools
import math

import jax
import jax.numpy as jnp
from jax import lax
from jax.experimental import pallas as pl
from jax.experimental.pallas import tpu as pltpu
from jax.sharding import PartitionSpec as P

MESH = pl.DeviceIdType.MESH
HIDDEN = -1e30
ID_ROWS = 16


def inner_size(mesh):
    axes = list(mesh.axis_names)
    column = mesh.devices if axes.index("ctx") == 0 else mesh.devices.T
    places = [getattr(device, "coords", None) for device in column[:, 0]]
    count = len(places)
    if count < 2 or any(place is None for place in places):
        return 1
    moved = [i for i in range(len(places[0])) if places[0][i] != places[1][i]]
    if len(moved) != 1:
        return 1
    inner = len({place[moved[0]] for place in places})
    return inner if count % (2 * inner) == 0 else 1


def kernel(
    outer, inner, heads,
    q_ref, k_ref, v_ref, id_ref, out_ref,
    kv, qs, top, acc, done, id_col,
    along_send, across_send, block_recv, out_send, out_recv,
):
    reach = outer // 2
    q_heads, rows, size = qs.shape
    kv_heads = kv.shape[2] // 2
    group = q_heads // kv_heads
    out_rows = out_ref.shape[0]
    pieces = 2 * kv_heads
    factor = size ** -0.5 * math.log2(math.e)

    me = lax.axis_index("ctx")
    a, b = me // inner, me % inner
    place = lax.axis_index("head")
    has_prev, has_next = a > 0, a < outer - 1

    def span(p):
        return pl.ds(0, rows + ID_ROWS) if p == 0 else pl.ds(0, rows)

    barrier = pltpu.get_barrier_semaphore()

    def greet(device_id):
        pl.semaphore_signal(barrier, inc=1, device_id=device_id, device_id_type=MESH)

    @pl.when(has_prev)
    def _():
        greet({"ctx": me - inner})

    @pl.when(has_next)
    def _():
        greet({"ctx": me + inner})

    for step in range(1, inner):
        greet({"ctx": a * inner + (b + step) % inner})
    for step in range(1, heads):
        greet({"head": (place + step) % heads})

    def split_heads(ref, count, store):
        chunk = min(256, ref.shape[0])
        tokens = chunk // count
        row = lax.broadcasted_iota(jnp.int32, (chunk, chunk), 0)
        col = lax.broadcasted_iota(jnp.int32, (chunk, chunk), 1)
        order = jnp.where(col == (row % tokens) * count + row // tokens, 1.0, 0.0).astype(jnp.bfloat16)
        for i in range(ref.shape[0] // chunk):
            part = ref[i * chunk:(i + 1) * chunk, :]
            moved = jnp.dot(order, part, preferred_element_type=jnp.float32).astype(jnp.bfloat16)
            for h in range(count):
                store(h, pl.ds(i * tokens, tokens), moved[h * tokens:(h + 1) * tokens])

    def store_k(h, where, value):
        kv[0, b, 2 * h, where, :] = value

    def store_v(h, where, value):
        kv[0, b, 2 * h + 1, where, :] = value

    def store_q(h, where, value):
        qs[h, where, :] = value

    split_heads(k_ref, kv_heads, store_k)
    split_heads(v_ref, kv_heads, store_v)
    numbers = id_ref[...].astype(jnp.float32)
    line = lax.broadcasted_iota(jnp.int32, (ID_ROWS, size), 0)
    lines = jnp.zeros((ID_ROWS, size), jnp.float32)
    for i in range(rows // size):
        lines = jnp.where(line == i, numbers[i:i + 1, :], lines)
    kv[0, b, 0, rows:rows + ID_ROWS, :] = lines.astype(jnp.bfloat16)

    greeted = has_prev.astype(jnp.int32) + has_next.astype(jnp.int32) + (inner - 1) + (heads - 1)
    pl.semaphore_wait(barrier, greeted)

    def along(da, p):
        return pltpu.make_async_remote_copy(
            src_ref=kv.at[da, b, p, span(p)],
            dst_ref=kv.at[da + 1, b, p, span(p)],
            send_sem=along_send.at[da, p],
            recv_sem=block_recv.at[da + 1, b, p],
            device_id={"ctx": me + inner},
            device_id_type=MESH,
        )

    def across(da, p, to):
        return pltpu.make_async_remote_copy(
            src_ref=kv.at[da, b, p, span(p)],
            dst_ref=kv.at[da, b, p, span(p)],
            send_sem=across_send.at[da, to, p],
            recv_sem=block_recv.at[da, b, p],
            device_id={"ctx": a * inner + to},
            device_id_type=MESH,
        )

    def landed(da, at, p):
        return pltpu.make_async_remote_copy(
            src_ref=kv.at[da, at, p, span(p)],
            dst_ref=kv.at[da, at, p, span(p)],
            send_sem=along_send.at[0, p],
            recv_sem=block_recv.at[da, at, p],
            device_id={"ctx": me},
            device_id_type=MESH,
        )

    def needed(da, src, dst):
        if da == 0:
            return src < dst
        if da == reach:
            return src > dst
        return src != dst

    def spread(da, p, act):
        if da < reach:
            @pl.when(has_next)
            def _():
                act(along(da, p))
        for step in range(1, inner):
            to = (b + step) % inner

            @pl.when(needed(da, b, to))
            def _():
                act(across(da, p, to))

    for p in range(pieces):
        spread(0, p, lambda copy: copy.start())

    split_heads(q_ref, q_heads, store_q)

    row = lax.broadcasted_iota(jnp.int32, (rows, rows), 0)
    col = lax.broadcasted_iota(jnp.int32, (rows, rows), 1)

    def key_ids(da, at):
        held = kv[da, at, 0, rows:rows + ID_ROWS, :].astype(jnp.float32)
        return jnp.concatenate([held[i:i + 1, :] for i in range(rows // size)], axis=1)

    own_ids = key_ids(0, b)
    column = jnp.sum(jnp.where(row == col, own_ids, 0.0), axis=1, keepdims=True)
    id_col[...] = jnp.broadcast_to(column, id_col.shape)

    def wide(value, width):
        return jnp.concatenate([value] * (width // value.shape[1]), axis=1)

    def attend(da, at, g, first=False):
        same = wide(id_col[...], rows) == key_ids(da, at)
        if first:
            same = same & (col <= row)
        bias = jnp.where(same, 0.0, HIDDEN)
        keys = kv[da, at, 2 * g, :rows, :]
        values = kv[da, at, 2 * g + 1, :rows, :]
        values = jnp.concatenate([values, jnp.ones_like(values)], axis=1)
        for j in range(group):
            h = g * group + j
            scores = lax.dot_general(
                qs[h], keys, (((1,), (1,)), ((), ())), preferred_element_type=jnp.float32
            ) + bias
            highest = jnp.broadcast_to(jnp.max(scores, axis=1, keepdims=True), (rows, size))
            if not first:
                old = top[h]
                highest = jnp.maximum(old, highest)
            weights = jnp.exp2((scores - wide(highest, rows)) * factor).astype(jnp.bfloat16)
            product = jnp.dot(weights, values, preferred_element_type=jnp.float32)
            if not first:
                product = acc[h] * wide(jnp.exp2((old - highest) * factor), 2 * size) + product
            top[h] = highest
            acc[h] = product

    def pass_on(da, g):
        @pl.when(a >= da)
        def _():
            for p in (2 * g, 2 * g + 1):
                landed(da, b, p).wait_recv()
                spread(da, p, lambda copy: copy.start())

    def column_block(da, g):
        @pl.when(a >= da)
        def _():
            attend(da, b, g)

    def inner_blocks(da, g):
        if inner == 1:
            return

        def one(step, carry):
            at = (b + step) % inner

            @pl.when((a >= da) & needed(da, at, b))
            def _():
                for p in (2 * g, 2 * g + 1):
                    landed(da, at, p).wait_recv()
                attend(da, at, g)

            return carry

        lax.fori_loop(1, inner, one, 0)

    def give(h, to):
        return pltpu.make_async_remote_copy(
            src_ref=done.at[h, pl.ds(to * out_rows, out_rows)],
            dst_ref=out_ref.at[:, pl.ds(pl.multiple_of((place * q_heads + h) * size, size), size)],
            send_sem=out_send.at[h, to],
            recv_sem=out_recv.at[h, place],
            device_id={"head": to},
            device_id_type=MESH,
        )

    def taken(h, source):
        return pltpu.make_async_remote_copy(
            src_ref=done.at[h, pl.ds(0, out_rows)],
            dst_ref=out_ref.at[:, pl.ds(pl.multiple_of((source * q_heads + h) * size, size), size)],
            send_sem=out_send.at[h, source],
            recv_sem=out_recv.at[h, source],
            device_id={"head": source},
            device_id_type=MESH,
        )

    def finish(g):
        for j in range(group):
            h = g * group + j
            total = acc[h]
            done[h] = (total[:, :size] / total[:, size:]).astype(jnp.bfloat16)
            for step in range(1, heads):
                give(h, (place + step) % heads).start()
        for j in range(group):
            h = g * group + j
            out_ref[:, pl.ds(pl.multiple_of((place * q_heads + h) * size, size), size)] = done[
                h, pl.ds(pl.multiple_of(place * out_rows, out_rows), out_rows), :
            ]

    groups = range(kv_heads)
    for g in groups:
        attend(0, b, g, first=True)
    for da in range(1, reach + 1):
        if da < reach:
            for g in groups:
                pass_on(da, g)
                column_block(da, g)
                inner_blocks(da - 1, g)
        else:
            for g in groups:
                pass_on(da, g)
                if g > 0:
                    inner_blocks(da, g - 1)
                    finish(g - 1)
                else:
                    for other in groups:
                        inner_blocks(da - 1, other)
                column_block(da, g)
            inner_blocks(da, kv_heads - 1)
            finish(kv_heads - 1)

    for h in range(q_heads):
        for step in range(1, heads):
            taken(h, (place + step) % heads).wait_recv()
    for da in range(reach + 1):
        @pl.when(a >= da)
        def _():
            for p in range(pieces):
                spread(da, p, lambda copy: copy.wait_send())
    for h in range(q_heads):
        for step in range(1, heads):
            give(h, (place + step) % heads).wait_send()


def local(outer, inner, heads, queries, keys, values, doc_ids):
    rows, q_heads, size = queries.shape
    kv_heads = keys.shape[1]
    reach = outer // 2
    return pl.pallas_call(
        functools.partial(kernel, outer, inner, heads),
        out_shape=jax.ShapeDtypeStruct((rows // heads, heads * q_heads * size), jnp.bfloat16),
        in_specs=[pl.BlockSpec(memory_space=pltpu.VMEM)] * 4,
        out_specs=pl.BlockSpec(memory_space=pltpu.VMEM),
        scratch_shapes=[
            pltpu.VMEM((reach + 1, inner, 2 * kv_heads, rows + ID_ROWS, size), jnp.bfloat16),
            pltpu.VMEM((q_heads, rows, size), jnp.bfloat16),
            pltpu.VMEM((q_heads, rows, size), jnp.float32),
            pltpu.VMEM((q_heads, rows, 2 * size), jnp.float32),
            pltpu.VMEM((q_heads, rows, size), jnp.bfloat16),
            pltpu.VMEM((rows, size), jnp.float32),
            pltpu.SemaphoreType.DMA((reach, 2 * kv_heads)),
            pltpu.SemaphoreType.DMA((reach + 1, inner, 2 * kv_heads)),
            pltpu.SemaphoreType.DMA((reach + 1, inner, 2 * kv_heads)),
            pltpu.SemaphoreType.DMA((q_heads, heads)),
            pltpu.SemaphoreType.DMA((q_heads, heads)),
        ],
        compiler_params=pltpu.CompilerParams(
            collective_id=0, has_side_effects=True, vmem_limit_bytes=48 * 1024 * 1024
        ),
    )(
        queries.reshape(rows * q_heads, size),
        keys.reshape(rows * kv_heads, size),
        values.reshape(rows * kv_heads, size),
        doc_ids.reshape(rows // size, size),
    )


def solution(mesh):
    inner = inner_size(mesh)
    return jax.shard_map(
        functools.partial(local, mesh.shape["ctx"] // inner, inner, mesh.shape["head"]),
        mesh=mesh,
        in_specs=(P("ctx", "head", None), P("ctx", "head", None), P("ctx", "head", None), P("ctx")),
        out_specs=P(("ctx", "head"), None),
        check_vma=False,
    )
```

time: 138 us -> 30.5 us (0.22)
  the two profiles are of different devices: /device:TPU:0 before, /device:TPU:17 now
where the time goes in v1:
time: 30.5 us; the launch traced here: 30.3 us
  Pallas kernels  26 us (85%)
  local copies, waits for them, and re-layouts  4.32 us (14%)
    pallas_call x1, Pallas kernels, local(): pl.pallas_call(functools.partial(kernel, outer, inner, heads), out_shape=...  26 us
    unnamed x9, local copies, waits for them, and re-layouts  4.32 us

profile of v1, /device:TPU:17, one launch (start us, length us, event | category | flops | bytes accessed | tf_op | source)
XLA Modules:
  0.0 30.3 jit_solution(12762671102467170820)
XLA Ops:
  0.0 0.0 copy-start.3
  0.0 0.7 %copy-done.3 = s32[256]{0:T(256)S(1)} copy-done((s32[256]{0:T(256)S(1)}, s32[256]{0:T(256)}, u32[]{:S(2)}) %copy-start.3) | copy-done | bytes 1048
  0.7 0.0 copy-start
  0.7 1.0 %copy-done = bf16[256,8,128]{2,1,0:T(8,128)(2,1)S(1)} copy-done((bf16[256,8,128]{2,1,0:T(8,128)(2,1)S(1)}, bf16[256,8,128]{2,1,0:T(8,128)(2,1)}, u32[]{:S(2)}) %copy-start) | copy-done | bytes 524312
  1.7 0.0 copy-start.1
  1.7 0.9 %copy-done.1 = bf16[256,2,128]{2,1,0:T(2,128)(2,1)S(1)} copy-done((bf16[256,2,128]{2,1,0:T(2,128)(2,1)S(1)}, bf16[256,2,128]{2,1,0:T(2,128)(2,1)}, u32[]{:S(2)}) %copy-start.1) | copy-done | bytes 131096
  2.6 0.0 copy-start.2
  2.6 0.9 %copy-done.2 = bf16[256,2,128]{2,1,0:T(2,128)(2,1)S(1)} copy-done((bf16[256,2,128]{2,1,0:T(2,128)(2,1)S(1)}, bf16[256,2,128]{2,1,0:T(2,128)(2,1)}, u32[]{:S(2)}) %copy-start.2) | copy-done | bytes 131096
  3.5 26.0 %shard_map.46 = bf16[64,4096]{1,0:T(8,128)(2,1)S(1)} custom-call(bf16[2048,128]{1,0:T(8,128)(2,1)S(1)} %bitcast.4, bf16[512,128]{1,0:T(8,128)(2,1)S(1)} %bitcast.5, bf16[512,128]{1,0:T(8,128)(2,1)S(1)} %bitcast.6, s32[2,128]{1,0:T(2,128)S(1)} %bitcast.7), custom_call_target="tpu_custom_call" | custom-call | tf_op jit(solution)/shard_map/pallas_call | solution.py:296
  29.5 0.8 %copy.6 = bf16[64,4096]{1,0:T(8,128)(2,1)} copy(bf16[64,4096]{1,0:T(8,128)(2,1)S(1)} %shard_map.46) | data formatting | bytes 1048576
Async XLA Ops:
  0.0 0.7 %copy-start.3 = (s32[256]{0:T(256)S(1)}, s32[256]{0:T(256)}, u32[]{:S(2)}) copy-start(s32[256]{0:T(256)} %param.7) | copy-start | bytes 3076
  0.7 1.0 %copy-start = (bf16[256,8,128]{2,1,0:T(8,128)(2,1)S(1)}, bf16[256,8,128]{2,1,0:T(8,128)(2,1)}, u32[]{:S(2)}) copy-start(bf16[256,8,128]{2,1,0:T(8,128)(2,1)} %param.4) | copy-start | bytes 1572868
  1.7 0.9 %copy-start.1 = (bf16[256,2,128]{2,1,0:T(2,128)(2,1)S(1)}, bf16[256,2,128]{2,1,0:T(2,128)(2,1)}, u32[]{:S(2)}) copy-start(bf16[256,2,128]{2,1,0:T(2,128)(2,1)} %param.5) | copy-start | bytes 393220
  2.6 0.9 %copy-start.2 = (bf16[256,2,128]{2,1,0:T(2,128)(2,1)S(1)}, bf16[256,2,128]{2,1,0:T(2,128)(2,1)}, u32[]{:S(2)}) copy-start(bf16[256,2,128]{2,1,0:T(2,128)(2,1)} %param.6) | copy-start | bytes 393220

commit v2 on v1

--- a/solution.py
+++ b/solution.py
@@ -29,8 +29,8 @@
 
 def kernel(
     outer, inner, heads,
-    q_ref, k_ref, v_ref, id_ref, out_ref,
-    kv, qs, top, acc, done, id_col,
+    q_hbm, k_hbm, v_hbm, id_hbm, out_ref,
+    q_ref, k_ref, v_ref, id_ref, loaded, kv, qs, top, acc, done, id_col,
     along_send, across_send, block_recv, out_send, out_recv,
 ):
     reach = outer // 2
@@ -48,6 +48,15 @@
 
     def span(p):
         return pl.ds(0, rows + ID_ROWS) if p == 0 else pl.ds(0, rows)
+
+    loads = [
+        pltpu.make_async_copy(source, held, loaded.at[i])
+        for i, (source, held) in enumerate(
+            ((k_hbm, k_ref), (v_hbm, v_ref), (id_hbm, id_ref), (q_hbm, q_ref))
+        )
+    ]
+    for load in loads:
+        load.start()
 
     barrier = pltpu.get_barrier_semaphore()
 
@@ -88,8 +97,11 @@
     def store_q(h, where, value):
         qs[h, where, :] = value
 
+    loads[0].wait()
     split_heads(k_ref, kv_heads, store_k)
+    loads[1].wait()
     split_heads(v_ref, kv_heads, store_v)
+    loads[2].wait()
     numbers = id_ref[...].astype(jnp.float32)
     line = lax.broadcasted_iota(jnp.int32, (ID_ROWS, size), 0)
     lines = jnp.zeros((ID_ROWS, size), jnp.float32)
@@ -152,6 +164,7 @@
     for p in range(pieces):
         spread(0, p, lambda copy: copy.start())
 
+    loads[3].wait()
     split_heads(q_ref, q_heads, store_q)
 
     row = lax.broadcasted_iota(jnp.int32, (rows, rows), 0)
@@ -192,10 +205,10 @@
             top[h] = highest
             acc[h] = product
 
-    def pass_on(da, g):
+    def pass_on(da, *which):
         @pl.when(a >= da)
         def _():
-            for p in (2 * g, 2 * g + 1):
+            for p in which:
                 landed(da, b, p).wait_recv()
                 spread(da, p, lambda copy: copy.start())
 
@@ -257,24 +270,23 @@
     groups = range(kv_heads)
     for g in groups:
         attend(0, b, g, first=True)
-    for da in range(1, reach + 1):
-        if da < reach:
-            for g in groups:
-                pass_on(da, g)
-                column_block(da, g)
-                inner_blocks(da - 1, g)
-        else:
-            for g in groups:
-                pass_on(da, g)
-                if g > 0:
-                    inner_blocks(da, g - 1)
-                    finish(g - 1)
-                else:
-                    for other in groups:
-                        inner_blocks(da - 1, other)
-                column_block(da, g)
-            inner_blocks(da, kv_heads - 1)
-            finish(kv_heads - 1)
+    for da in range(1, reach):
+        pass_on(da, 0, 1)
+        for g in groups:
+            column_block(da, g)
+            if g + 1 < kv_heads:
+                pass_on(da, 2 * g + 2, 2 * g + 3)
+            inner_blocks(da - 1, g)
+    for g in groups:
+        pass_on(reach, 2 * g)
+        inner_blocks(reach - 1, g)
+        pass_on(reach, 2 * g + 1)
+        if g > 0:
+            inner_blocks(reach, g - 1)
+            finish(g - 1)
+        column_block(reach, g)
+    inner_blocks(reach, kv_heads - 1)
+    finish(kv_heads - 1)
 
     for h in range(q_heads):
         for step in range(1, heads):
@@ -289,6 +301,10 @@
             give(h, (place + step) % heads).wait_send()
 
 
+def in_hbm(array):
+    return pltpu.with_memory_space_constraint(array, pltpu.HBM)
+
+
 def local(outer, inner, heads, queries, keys, values, doc_ids):
     rows, q_heads, size = queries.shape
     kv_heads = keys.shape[1]
@@ -296,9 +312,14 @@
     return pl.pallas_call(
         functools.partial(kernel, outer, inner, heads),
         out_shape=jax.ShapeDtypeStruct((rows // heads, heads * q_heads * size), jnp.bfloat16),
-        in_specs=[pl.BlockSpec(memory_space=pltpu.VMEM)] * 4,
+        in_specs=[pl.BlockSpec(memory_space=pltpu.HBM)] * 4,
         out_specs=pl.BlockSpec(memory_space=pltpu.VMEM),
         scratch_shapes=[
+            pltpu.VMEM((rows * q_heads, size), jnp.bfloat16),
+            pltpu.VMEM((rows * kv_heads, size), jnp.bfloat16),
+            pltpu.VMEM((rows * kv_heads, size), jnp.bfloat16),
+            pltpu.VMEM((rows // size, size), jnp.int32),
+            pltpu.SemaphoreType.DMA((4,)),
             pltpu.VMEM((reach + 1, inner, 2 * kv_heads, rows + ID_ROWS, size), jnp.bfloat16),
             pltpu.VMEM((q_heads, rows, size), jnp.bfloat16),
             pltpu.VMEM((q_heads, rows, size), jnp.float32),
@@ -315,10 +336,10 @@
             collective_id=0, has_side_effects=True, vmem_limit_bytes=48 * 1024 * 1024
         ),
     )(
-        queries.reshape(rows * q_heads, size),
-        keys.reshape(rows * kv_heads, size),
-        values.reshape(rows * kv_heads, size),
-        doc_ids.reshape(rows // size, size),
+        in_hbm(queries.reshape(rows * q_heads, size)),
+        in_hbm(keys.reshape(rows * kv_heads, size)),
+        in_hbm(values.reshape(rows * kv_heads, size)),
+        in_hbm(doc_ids.reshape(rows // size, size)),
     )
 
 

time: 30.5 us -> 27 us (0.89)
  local copies, waits for them, and re-layouts: 4.32 us -> 0.8 us
    unnamed x9 -> x1, local copies, waits for them, and re-layouts: 4.32 us -> 0.8 us
where the time goes in v2:
time: 27 us; the launch traced here: 26.8 us
  Pallas kernels  26 us (96%)
  local copies, waits for them, and re-layouts  0.8 us (3%)
    pallas_call x1, Pallas kernels, local(): pl.pallas_call(functools.partial(kernel, outer, inner, heads), out_shape=...  26 us
    unnamed x1, local copies, waits for them, and re-layouts  0.8 us

profile of v2, /device:TPU:17, one launch (start us, length us, event | category | flops | bytes accessed | tf_op | source)
XLA Modules:
  0.0 26.8 jit_solution(18374057969166569265)
XLA Ops:
  0.0 26.0 %shard_map.46 = bf16[64,4096]{1,0:T(8,128)(2,1)S(1)} custom-call(bf16[2048,128]{1,0:T(8,128)(2,1)} %bitcast.4, bf16[512,128]{1,0:T(8,128)(2,1)} %bitcast.5, bf16[512,128]{1,0:T(8,128)(2,1)} %bitcast.6, s32[2,128]{1,0:T(2,128)} %bitcast.7), custom_call_target="tpu_custom_call" | custom-call | tf_op jit(solution)/shard_map/pallas_call | solution.py:312
  26.0 0.8 %copy.6 = bf16[64,4096]{1,0:T(8,128)(2,1)} copy(bf16[64,4096]{1,0:T(8,128)(2,1)S(1)} %shard_map.46) | data formatting | bytes 1048576

commit v3 on v2

--- a/solution.py
+++ b/solution.py
@@ -275,18 +275,33 @@
         for g in groups:
             column_block(da, g)
             if g + 1 < kv_heads:
+                inner_blocks(da - 1, g)
                 pass_on(da, 2 * g + 2, 2 * g + 3)
-            inner_blocks(da - 1, g)
-    for g in groups:
-        pass_on(reach, 2 * g)
-        inner_blocks(reach - 1, g)
-        pass_on(reach, 2 * g + 1)
-        if g > 0:
-            inner_blocks(reach, g - 1)
-            finish(g - 1)
-        column_block(reach, g)
-    inner_blocks(reach, kv_heads - 1)
-    finish(kv_heads - 1)
+            else:
+                inner_blocks(da - 1, g)
+
+    @pl.when(b > 0)
+    def _():
+        pass_on(reach, 0, 1)
+        for g in groups:
+            column_block(reach, g)
+            if g + 1 < kv_heads:
+                pass_on(reach, 2 * g + 2)
+            inner_blocks(reach - 1, g)
+            if g + 1 < kv_heads:
+                pass_on(reach, 2 * g + 3)
+            inner_blocks(reach, g)
+            finish(g)
+
+    @pl.when(b == 0)
+    def _():
+        for g in groups:
+            inner_blocks(reach - 1, g)
+        for g in groups:
+            pass_on(reach, 2 * g, 2 * g + 1)
+            column_block(reach, g)
+            inner_blocks(reach, g)
+            finish(g)
 
     for h in range(q_heads):
         for step in range(1, heads):

time: 27 us -> 26.3 us (0.974)
  Pallas kernels: 26 us -> 25.3 us
    pallas_call x1, Pallas kernels: 26 us -> 25.3 us  [local(): pl.pallas_call(functools.partial(kernel, outer, inner, heads), out_shape=...]
where the time goes in v3:
time: 26.3 us; the launch traced here: 26.1 us
  Pallas kernels  25.3 us (96%)
  local copies, waits for them, and re-layouts  0.8 us (3%)
    pallas_call x1, Pallas kernels, local(): pl.pallas_call(functools.partial(kernel, outer, inner, heads), out_shape=...  25.3 us
    unnamed x1, local copies, waits for them, and re-layouts  0.8 us

profile of v3, /device:TPU:17, one launch (start us, length us, event | category | flops | bytes accessed | tf_op | source)
XLA Modules:
  0.0 26.1 jit_solution(438011171518393266)
XLA Ops:
  0.0 25.3 %shard_map.46 = bf16[64,4096]{1,0:T(8,128)(2,1)S(1)} custom-call(bf16[2048,128]{1,0:T(8,128)(2,1)} %bitcast.4, bf16[512,128]{1,0:T(8,128)(2,1)} %bitcast.5, bf16[512,128]{1,0:T(8,128)(2,1)} %bitcast.6, s32[2,128]{1,0:T(2,128)} %bitcast.7), custom_call_target="tpu_custom_call" | custom-call | tf_op jit(solution)/shard_map/pallas_call | solution.py:327
  25.3 0.8 %copy.6 = bf16[64,4096]{1,0:T(8,128)(2,1)} copy(bf16[64,4096]{1,0:T(8,128)(2,1)S(1)} %shard_map.46) | data formatting | bytes 1048576

commit v4 on v3

--- a/solution.py
+++ b/solution.py
@@ -30,8 +30,8 @@
 def kernel(
     outer, inner, heads,
     q_hbm, k_hbm, v_hbm, id_hbm, out_ref,
-    q_ref, k_ref, v_ref, id_ref, loaded, kv, qs, top, acc, done, id_col,
-    along_send, across_send, block_recv, out_send, out_recv,
+    q_ref, k_ref, v_ref, id_ref, loaded, kv, qs, top, acc, probs, done, id_col,
+    along_send, across_send, direct_send, block_recv, out_send, out_recv,
 ):
     reach = outer // 2
     q_heads, rows, size = qs.shape
@@ -75,6 +75,15 @@
         greet({"ctx": a * inner + (b + step) % inner})
     for step in range(1, heads):
         greet({"head": (place + step) % heads})
+
+    for step in range(1, inner):
+        @pl.when(has_next & (step <= b))
+        def _():
+            greet({"ctx": me + inner - step})
+
+        @pl.when(has_prev & (b + step < inner))
+        def _():
+            greet({"ctx": me - inner + step})
 
     def split_heads(ref, count, store):
         chunk = min(256, ref.shape[0])
@@ -109,7 +118,8 @@
         lines = jnp.where(line == i, numbers[i:i + 1, :], lines)
     kv[0, b, 0, rows:rows + ID_ROWS, :] = lines.astype(jnp.bfloat16)
 
-    greeted = has_prev.astype(jnp.int32) + has_next.astype(jnp.int32) + (inner - 1) + (heads - 1)
+    up, down = has_next.astype(jnp.int32), has_prev.astype(jnp.int32)
+    greeted = up * (1 + b) + down * (inner - b) + (inner - 1) + (heads - 1)
     pl.semaphore_wait(barrier, greeted)
 
     def along(da, p):
@@ -129,6 +139,17 @@
             send_sem=across_send.at[da, to, p],
             recv_sem=block_recv.at[da, b, p],
             device_id={"ctx": a * inner + to},
+            device_id_type=MESH,
+        )
+
+    def direct(step):
+        p = pieces - 1
+        return pltpu.make_async_remote_copy(
+            src_ref=kv.at[reach - 1, b, p, span(p)],
+            dst_ref=kv.at[reach, b, p, span(p)],
+            send_sem=direct_send.at[step],
+            recv_sem=block_recv.at[reach, b, p],
+            device_id={"ctx": me + inner - step},
             device_id_type=MESH,
         )
 
@@ -156,6 +177,12 @@
                 act(along(da, p))
         for step in range(1, inner):
             to = (b + step) % inner
+            if p == pieces - 1 and da == reach - 1:
+                @pl.when(has_next & (step <= b))
+                def _():
+                    act(direct(step))
+            if p == pieces - 1 and da == reach:
+                continue
 
             @pl.when(needed(da, b, to))
             def _():
@@ -205,6 +232,30 @@
             top[h] = highest
             acc[h] = product
 
+    def attend_last(da, at, g):
+        landed(da, at, 2 * g).wait_recv()
+        bias = jnp.where(wide(id_col[...], rows) == key_ids(da, at), 0.0, HIDDEN)
+        keys = kv[da, at, 2 * g, :rows, :]
+        for j in range(group):
+            h = g * group + j
+            scores = lax.dot_general(
+                qs[h], keys, (((1,), (1,)), ((), ())), preferred_element_type=jnp.float32
+            ) + bias
+            old = top[h]
+            highest = jnp.maximum(
+                old, jnp.broadcast_to(jnp.max(scores, axis=1, keepdims=True), (rows, size))
+            )
+            probs[j] = jnp.exp2((scores - wide(highest, rows)) * factor).astype(jnp.bfloat16)
+            top[h] = jnp.exp2((old - highest) * factor)
+        landed(da, at, 2 * g + 1).wait_recv()
+        values = kv[da, at, 2 * g + 1, :rows, :]
+        values = jnp.concatenate([values, jnp.ones_like(values)], axis=1)
+        for j in range(group):
+            h = g * group + j
+            product = jnp.dot(probs[j], values, preferred_element_type=jnp.float32)
+            close(h, acc[h] * wide(top[h], 2 * size) + product)
+        keep(g)
+
     def pass_on(da, *which):
         @pl.when(a >= da)
         def _():
@@ -217,7 +268,11 @@
         def _():
             attend(da, b, g)
 
-    def inner_blocks(da, g):
+    def inner_blocks(da, g, last=False):
+        if last:
+            steps = inner - 1
+        else:
+            steps = inner
         if inner == 1:
             return
 
@@ -232,7 +287,16 @@
 
             return carry
 
-        lax.fori_loop(1, inner, one, 0)
+        if steps > 1:
+            lax.fori_loop(1, steps, one, 0)
+        if last:
+            @pl.when(a >= da)
+            def _():
+                attend_last(da, (b + inner - 1) % inner, g)
+
+            @pl.when(a < da)
+            def _():
+                finish(g)
 
     def give(h, to):
         return pltpu.make_async_remote_copy(
@@ -254,18 +318,22 @@
             device_id_type=MESH,
         )
 
-    def finish(g):
-        for j in range(group):
-            h = g * group + j
-            total = acc[h]
-            done[h] = (total[:, :size] / total[:, size:]).astype(jnp.bfloat16)
-            for step in range(1, heads):
-                give(h, (place + step) % heads).start()
+    def close(h, total):
+        done[h] = (total[:, :size] / total[:, size:]).astype(jnp.bfloat16)
+        for step in range(1, heads):
+            give(h, (place + step) % heads).start()
+
+    def keep(g):
         for j in range(group):
             h = g * group + j
             out_ref[:, pl.ds(pl.multiple_of((place * q_heads + h) * size, size), size)] = done[
                 h, pl.ds(pl.multiple_of(place * out_rows, out_rows), out_rows), :
             ]
+
+    def finish(g):
+        for j in range(group):
+            close(g * group + j, acc[g * group + j])
+        keep(g)
 
     groups = range(kv_heads)
     for g in groups:
@@ -286,12 +354,13 @@
         for g in groups:
             column_block(reach, g)
             if g + 1 < kv_heads:
-                pass_on(reach, 2 * g + 2)
-            inner_blocks(reach - 1, g)
-            if g + 1 < kv_heads:
-                pass_on(reach, 2 * g + 3)
+                pass_on(reach, 2 * g + 2, 2 * g + 3)
             inner_blocks(reach, g)
-            finish(g)
+            if reach > 1 and inner > 1:
+                inner_blocks(reach - 1, g, last=True)
+            else:
+                inner_blocks(reach - 1, g)
+                finish(g)
 
     @pl.when(b == 0)
     def _():
@@ -300,8 +369,10 @@
         for g in groups:
             pass_on(reach, 2 * g, 2 * g + 1)
             column_block(reach, g)
-            inner_blocks(reach, g)
-            finish(g)
+            if inner > 1:
+                inner_blocks(reach, g, last=True)
+            else:
+                finish(g)
 
     for h in range(q_heads):
         for step in range(1, heads):
@@ -339,10 +410,12 @@
             pltpu.VMEM((q_heads, rows, size), jnp.bfloat16),
             pltpu.VMEM((q_heads, rows, size), jnp.float32),
             pltpu.VMEM((q_heads, rows, 2 * size), jnp.float32),
+            pltpu.VMEM((q_heads // kv_heads, rows, rows), jnp.bfloat16),
             pltpu.VMEM((q_heads, rows, size), jnp.bfloat16),
             pltpu.VMEM((rows, size), jnp.float32),
             pltpu.SemaphoreType.DMA((reach, 2 * kv_heads)),
             pltpu.SemaphoreType.DMA((reach + 1, inner, 2 * kv_heads)),
+            pltpu.SemaphoreType.DMA((inner,)),
             pltpu.SemaphoreType.DMA((reach + 1, inner, 2 * kv_heads)),
             pltpu.SemaphoreType.DMA((q_heads, heads)),
             pltpu.SemaphoreType.DMA((q_heads, heads)),

time: 26.3 us -> 26.3 us (level)
  no operation moved by 1% of the time
where the time goes in v4:
time: 26.3 us; the launch traced here: 26.1 us
  Pallas kernels  25.3 us (96%)
  local copies, waits for them, and re-layouts  0.8 us (3%)
    pallas_call x1, Pallas kernels, local(): pl.pallas_call(functools.partial(kernel, outer, inner, heads), out_shape=...  25.3 us
    unnamed x1, local copies, waits for them, and re-layouts  0.8 us

profile of v4, /device:TPU:17, one launch (start us, length us, event | category | flops | bytes accessed | tf_op | source)
XLA Modules:
  0.0 26.1 jit_solution(14485079745998263479)
XLA Ops:
  0.0 25.3 %shard_map.46 = bf16[64,4096]{1,0:T(8,128)(2,1)S(1)} custom-call(bf16[2048,128]{1,0:T(8,128)(2,1)} %bitcast.4, bf16[512,128]{1,0:T(8,128)(2,1)} %bitcast.5, bf16[512,128]{1,0:T(8,128)(2,1)} %bitcast.6, s32[2,128]{1,0:T(2,128)} %bitcast.7), custom_call_target="tpu_custom_call" | custom-call | tf_op jit(solution)/shard_map/pallas_call | solution.py:398
  25.3 0.8 %copy.6 = bf16[64,4096]{1,0:T(8,128)(2,1)} copy(bf16[64,4096]{1,0:T(8,128)(2,1)S(1)} %shard_map.46) | data formatting | bytes 1048576

commit v5 on v3

--- a/solution.py
+++ b/solution.py
@@ -10,6 +10,7 @@
 
 MESH = pl.DeviceIdType.MESH
 HIDDEN = -1e30
+ONE_ROWS = 16
 ID_ROWS = 16
 
 
@@ -30,12 +31,12 @@
 def kernel(
     outer, inner, heads,
     q_hbm, k_hbm, v_hbm, id_hbm, out_ref,
-    q_ref, k_ref, v_ref, id_ref, loaded, kv, qs, top, acc, done, id_col,
+    q_ref, k_ref, v_ref, id_ref, loaded, ks, vs, qs, top, acc, done,
     along_send, across_send, block_recv, out_send, out_recv,
 ):
     reach = outer // 2
     q_heads, rows, size = qs.shape
-    kv_heads = kv.shape[2] // 2
+    kv_heads = ks.shape[2]
     group = q_heads // kv_heads
     out_rows = out_ref.shape[0]
     pieces = 2 * kv_heads
@@ -46,8 +47,10 @@
     place = lax.axis_index("head")
     has_prev, has_next = a > 0, a < outer - 1
 
-    def span(p):
-        return pl.ds(0, rows + ID_ROWS) if p == 0 else pl.ds(0, rows)
+    def block(da, at, p):
+        if p % 2:
+            return vs.at[da, at, p // 2]
+        return ks.at[da, at, p // 2, pl.ds(0, rows + ID_ROWS if p == 0 else rows)]
 
     loads = [
         pltpu.make_async_copy(source, held, loaded.at[i])
@@ -84,18 +87,18 @@
         order = jnp.where(col == (row % tokens) * count + row // tokens, 1.0, 0.0).astype(jnp.bfloat16)
         for i in range(ref.shape[0] // chunk):
             part = ref[i * chunk:(i + 1) * chunk, :]
-            moved = jnp.dot(order, part, preferred_element_type=jnp.float32).astype(jnp.bfloat16)
+            moved = jnp.dot(order, part, preferred_element_type=jnp.float32)
             for h in range(count):
                 store(h, pl.ds(i * tokens, tokens), moved[h * tokens:(h + 1) * tokens])
 
     def store_k(h, where, value):
-        kv[0, b, 2 * h, where, :] = value
+        ks[0, b, h, where, :] = value.astype(jnp.bfloat16)
 
     def store_v(h, where, value):
-        kv[0, b, 2 * h + 1, where, :] = value
+        vs[0, b, h, :, where] = value.T.astype(jnp.bfloat16)
 
     def store_q(h, where, value):
-        qs[h, where, :] = value
+        qs[h, where, :] = value.astype(jnp.bfloat16)
 
     loads[0].wait()
     split_heads(k_ref, kv_heads, store_k)
@@ -107,15 +110,15 @@
     lines = jnp.zeros((ID_ROWS, size), jnp.float32)
     for i in range(rows // size):
         lines = jnp.where(line == i, numbers[i:i + 1, :], lines)
-    kv[0, b, 0, rows:rows + ID_ROWS, :] = lines.astype(jnp.bfloat16)
+    ks[0, b, 0, rows:rows + ID_ROWS, :] = lines.astype(jnp.bfloat16)
 
     greeted = has_prev.astype(jnp.int32) + has_next.astype(jnp.int32) + (inner - 1) + (heads - 1)
     pl.semaphore_wait(barrier, greeted)
 
     def along(da, p):
         return pltpu.make_async_remote_copy(
-            src_ref=kv.at[da, b, p, span(p)],
-            dst_ref=kv.at[da + 1, b, p, span(p)],
+            src_ref=block(da, b, p),
+            dst_ref=block(da + 1, b, p),
             send_sem=along_send.at[da, p],
             recv_sem=block_recv.at[da + 1, b, p],
             device_id={"ctx": me + inner},
@@ -124,8 +127,8 @@
 
     def across(da, p, to):
         return pltpu.make_async_remote_copy(
-            src_ref=kv.at[da, b, p, span(p)],
-            dst_ref=kv.at[da, b, p, span(p)],
+            src_ref=block(da, b, p),
+            dst_ref=block(da, b, p),
             send_sem=across_send.at[da, to, p],
             recv_sem=block_recv.at[da, b, p],
             device_id={"ctx": a * inner + to},
@@ -134,8 +137,8 @@
 
     def landed(da, at, p):
         return pltpu.make_async_remote_copy(
-            src_ref=kv.at[da, at, p, span(p)],
-            dst_ref=kv.at[da, at, p, span(p)],
+            src_ref=block(da, at, p),
+            dst_ref=block(da, at, p),
             send_sem=along_send.at[0, p],
             recv_sem=block_recv.at[da, at, p],
             device_id={"ctx": me},
@@ -170,38 +173,31 @@
     row = lax.broadcasted_iota(jnp.int32, (rows, rows), 0)
     col = lax.broadcasted_iota(jnp.int32, (rows, rows), 1)
 
-    def key_ids(da, at):
-        held = kv[da, at, 0, rows:rows + ID_ROWS, :].astype(jnp.float32)
+    def ids_line(da, at):
+        held = ks[da, at, 0, rows:rows + ID_ROWS, :].astype(jnp.float32)
         return jnp.concatenate([held[i:i + 1, :] for i in range(rows // size)], axis=1)
 
-    own_ids = key_ids(0, b)
-    column = jnp.sum(jnp.where(row == col, own_ids, 0.0), axis=1, keepdims=True)
-    id_col[...] = jnp.broadcast_to(column, id_col.shape)
-
-    def wide(value, width):
-        return jnp.concatenate([value] * (width // value.shape[1]), axis=1)
-
     def attend(da, at, g, first=False):
-        same = wide(id_col[...], rows) == key_ids(da, at)
+        key_ids = jnp.sum(jnp.where(row == col, ids_line(da, at), 0.0), axis=1, keepdims=True)
+        same = key_ids == ids_line(0, b)
         if first:
-            same = same & (col <= row)
+            same = same & (row <= col)
         bias = jnp.where(same, 0.0, HIDDEN)
-        keys = kv[da, at, 2 * g, :rows, :]
-        values = kv[da, at, 2 * g + 1, :rows, :]
-        values = jnp.concatenate([values, jnp.ones_like(values)], axis=1)
+        keys = ks[da, at, g, :rows, :]
+        values = jnp.concatenate([vs[da, at, g], jnp.ones((ONE_ROWS, rows), jnp.bfloat16)], axis=0)
         for j in range(group):
             h = g * group + j
             scores = lax.dot_general(
-                qs[h], keys, (((1,), (1,)), ((), ())), preferred_element_type=jnp.float32
+                keys, qs[h], (((1,), (1,)), ((), ())), preferred_element_type=jnp.float32
             ) + bias
-            highest = jnp.broadcast_to(jnp.max(scores, axis=1, keepdims=True), (rows, size))
+            highest = jnp.max(scores, axis=0, keepdims=True)
             if not first:
                 old = top[h]
                 highest = jnp.maximum(old, highest)
-            weights = jnp.exp2((scores - wide(highest, rows)) * factor).astype(jnp.bfloat16)
-            product = jnp.dot(weights, values, preferred_element_type=jnp.float32)
+            weights = jnp.exp2((scores - highest) * factor).astype(jnp.bfloat16)
+            product = jnp.dot(values, weights, preferred_element_type=jnp.float32)
             if not first:
-                product = acc[h] * wide(jnp.exp2((old - highest) * factor), 2 * size) + product
+                product = acc[h] * jnp.exp2((old - highest) * factor) + product
             top[h] = highest
             acc[h] = product
 
@@ -258,7 +254,7 @@
         for j in range(group):
             h = g * group + j
             total = acc[h]
-            done[h] = (total[:, :size] / total[:, size:]).astype(jnp.bfloat16)
+            done[h] = (total[:size] / total[size:size + 1]).T.astype(jnp.bfloat16)
             for step in range(1, heads):
                 give(h, (place + step) % heads).start()
         for j in range(group):
@@ -335,12 +331,12 @@
             pltpu.VMEM((rows * kv_heads, size), jnp.bfloat16),
             pltpu.VMEM((rows // size, size), jnp.int32),
             pltpu.SemaphoreType.DMA((4,)),
-            pltpu.VMEM((reach + 1, inner, 2 * kv_heads, rows + ID_ROWS, size), jnp.bfloat16),
+            pltpu.VMEM((reach + 1, inner, kv_heads, rows + ID_ROWS, size), jnp.bfloat16),
+            pltpu.VMEM((reach + 1, inner, kv_heads, size, rows), jnp.bfloat16),
             pltpu.VMEM((q_heads, rows, size), jnp.bfloat16),
-            pltpu.VMEM((q_heads, rows, size), jnp.float32),
-            pltpu.VMEM((q_heads, rows, 2 * size), jnp.float32),
+            pltpu.VMEM((q_heads, 1, rows), jnp.float32),
+            pltpu.VMEM((q_heads, size + ONE_ROWS, rows), jnp.float32),
             pltpu.VMEM((q_heads, rows, size), jnp.bfloat16),
-            pltpu.VMEM((rows, size), jnp.float32),
             pltpu.SemaphoreType.DMA((reach, 2 * kv_heads)),
             pltpu.SemaphoreType.DMA((reach + 1, inner, 2 * kv_heads)),
             pltpu.SemaphoreType.DMA((reach + 1, inner, 2 * kv_heads)),

time: 26.3 us -> 28.9 us (1.099)
  Pallas kernels: 25.3 us -> 27.9 us
    pallas_call x1, Pallas kernels: 25.3 us -> 27.9 us  [local(): pl.pallas_call(functools.partial(kernel, outer, inner, heads), out_shape=...]
where the time goes in v5:
time: 28.9 us; the launch traced here: 28.7 us
  Pallas kernels  27.9 us (97%)
  local copies, waits for them, and re-layouts  0.8 us (3%)
    pallas_call x1, Pallas kernels, local(): pl.pallas_call(functools.partial(kernel, outer, inner, heads), out_shape=...  27.9 us
    unnamed x1, local copies, waits for them, and re-layouts  0.8 us

profile of v5, /device:TPU:17, one launch (start us, length us, event | category | flops | bytes accessed | tf_op | source)
XLA Modules:
  0.0 28.7 jit_solution(6857284552312787653)
XLA Ops:
  0.0 27.9 %shard_map.46 = bf16[64,4096]{1,0:T(8,128)(2,1)S(1)} custom-call(bf16[2048,128]{1,0:T(8,128)(2,1)} %bitcast.4, bf16[512,128]{1,0:T(8,128)(2,1)} %bitcast.5, bf16[512,128]{1,0:T(8,128)(2,1)} %bitcast.6, s32[2,128]{1,0:T(2,128)} %bitcast.7), custom_call_target="tpu_custom_call" | custom-call | tf_op jit(solution)/shard_map/pallas_call | solution.py:323
  27.9 0.8 %copy.6 = bf16[64,4096]{1,0:T(8,128)(2,1)} copy(bf16[64,4096]{1,0:T(8,128)(2,1)S(1)} %shard_map.46) | data formatting | bytes 1048576

commit v6 on v2

--- a/solution.py
+++ b/solution.py
@@ -38,7 +38,6 @@
     kv_heads = kv.shape[2] // 2
     group = q_heads // kv_heads
     out_rows = out_ref.shape[0]
-    pieces = 2 * kv_heads
     factor = size ** -0.5 * math.log2(math.e)
 
     me = lax.axis_index("ctx")
@@ -46,8 +45,8 @@
     place = lax.axis_index("head")
     has_prev, has_next = a > 0, a < outer - 1
 
-    def span(p):
-        return pl.ds(0, rows + ID_ROWS) if p == 0 else pl.ds(0, rows)
+    def span(kind):
+        return pl.ds(0, rows + ID_ROWS) if kind == 0 else pl.ds(0, rows)
 
     loads = [
         pltpu.make_async_copy(source, held, loaded.at[i])
@@ -107,35 +106,41 @@
     lines = jnp.zeros((ID_ROWS, size), jnp.float32)
     for i in range(rows // size):
         lines = jnp.where(line == i, numbers[i:i + 1, :], lines)
-    kv[0, b, 0, rows:rows + ID_ROWS, :] = lines.astype(jnp.bfloat16)
+    for g in range(kv_heads):
+        kv[0, b, 2 * g, rows:rows + ID_ROWS, :] = lines.astype(jnp.bfloat16)
+    top[...] = jnp.full(top.shape, HIDDEN, jnp.float32)
+    acc[...] = jnp.zeros(acc.shape, jnp.float32)
 
     greeted = has_prev.astype(jnp.int32) + has_next.astype(jnp.int32) + (inner - 1) + (heads - 1)
     pl.semaphore_wait(barrier, greeted)
 
-    def along(da, p):
-        return pltpu.make_async_remote_copy(
-            src_ref=kv.at[da, b, p, span(p)],
-            dst_ref=kv.at[da + 1, b, p, span(p)],
+    def along(da, g, kind):
+        p = 2 * g + kind
+        return pltpu.make_async_remote_copy(
+            src_ref=kv.at[da, b, p, span(kind)],
+            dst_ref=kv.at[da + 1, b, p, span(kind)],
             send_sem=along_send.at[da, p],
             recv_sem=block_recv.at[da + 1, b, p],
             device_id={"ctx": me + inner},
             device_id_type=MESH,
         )
 
-    def across(da, p, to):
-        return pltpu.make_async_remote_copy(
-            src_ref=kv.at[da, b, p, span(p)],
-            dst_ref=kv.at[da, b, p, span(p)],
+    def across(da, g, kind, to):
+        p = 2 * g + kind
+        return pltpu.make_async_remote_copy(
+            src_ref=kv.at[da, b, p, span(kind)],
+            dst_ref=kv.at[da, b, p, span(kind)],
             send_sem=across_send.at[da, to, p],
             recv_sem=block_recv.at[da, b, p],
             device_id={"ctx": a * inner + to},
             device_id_type=MESH,
         )
 
-    def landed(da, at, p):
-        return pltpu.make_async_remote_copy(
-            src_ref=kv.at[da, at, p, span(p)],
-            dst_ref=kv.at[da, at, p, span(p)],
+    def landed(da, at, g, kind):
+        p = 2 * g + kind
+        return pltpu.make_async_remote_copy(
+            src_ref=kv.at[da, at, p, span(kind)],
+            dst_ref=kv.at[da, at, p, span(kind)],
             send_sem=along_send.at[0, p],
             recv_sem=block_recv.at[da, at, p],
             device_id={"ctx": me},
@@ -143,26 +148,23 @@
         )
 
     def needed(da, src, dst):
-        if da == 0:
-            return src < dst
-        if da == reach:
-            return src > dst
-        return src != dst
-
-    def spread(da, p, act):
-        if da < reach:
-            @pl.when(has_next)
-            def _():
-                act(along(da, p))
+        return (src != dst) & ((da > 0) | (src < dst)) & ((da < reach) | (src > dst))
+
+    def spread(da, g, kind, act):
+        @pl.when(has_next & (da < reach))
+        def _():
+            act(along(da, g, kind))
+
         for step in range(1, inner):
             to = (b + step) % inner
 
             @pl.when(needed(da, b, to))
             def _():
-                act(across(da, p, to))
-
-    for p in range(pieces):
-        spread(0, p, lambda copy: copy.start())
+                act(across(da, g, kind, to))
+
+    for g in range(kv_heads):
+        for kind in range(2):
+            spread(0, g, kind, lambda copy: copy.start())
 
     loads[3].wait()
     split_heads(q_ref, q_heads, store_q)
@@ -181,11 +183,10 @@
     def wide(value, width):
         return jnp.concatenate([value] * (width // value.shape[1]), axis=1)
 
-    def attend(da, at, g, first=False):
-        same = wide(id_col[...], rows) == key_ids(da, at)
-        if first:
-            same = same & (col <= row)
-        bias = jnp.where(same, 0.0, HIDDEN)
+    def attend(da, at, g):
+        back = (me - (a - da) * inner - at) * rows
+        visible = (wide(id_col[...], rows) == key_ids(da, at)) & (col - row <= back)
+        bias = jnp.where(visible, 0.0, HIDDEN)
         keys = kv[da, at, 2 * g, :rows, :]
         values = kv[da, at, 2 * g + 1, :rows, :]
         values = jnp.concatenate([values, jnp.ones_like(values)], axis=1)
@@ -194,45 +195,14 @@
             scores = lax.dot_general(
                 qs[h], keys, (((1,), (1,)), ((), ())), preferred_element_type=jnp.float32
             ) + bias
-            highest = jnp.broadcast_to(jnp.max(scores, axis=1, keepdims=True), (rows, size))
-            if not first:
-                old = top[h]
-                highest = jnp.maximum(old, highest)
+            old = top[h]
+            highest = jnp.maximum(
+                old, jnp.broadcast_to(jnp.max(scores, axis=1, keepdims=True), (rows, size))
+            )
             weights = jnp.exp2((scores - wide(highest, rows)) * factor).astype(jnp.bfloat16)
             product = jnp.dot(weights, values, preferred_element_type=jnp.float32)
-            if not first:
-                product = acc[h] * wide(jnp.exp2((old - highest) * factor), 2 * size) + product
+            acc[h] = acc[h] * wide(jnp.exp2((old - highest) * factor), 2 * size) + product
             top[h] = highest
-            acc[h] = product
-
-    def pass_on(da, *which):
-        @pl.when(a >= da)
-        def _():
-            for p in which:
-                landed(da, b, p).wait_recv()
-                spread(da, p, lambda copy: copy.start())
-
-    def column_block(da, g):
-        @pl.when(a >= da)
-        def _():
-            attend(da, b, g)
-
-    def inner_blocks(da, g):
-        if inner == 1:
-            return
-
-        def one(step, carry):
-            at = (b + step) % inner
-
-            @pl.when((a >= da) & needed(da, at, b))
-            def _():
-                for p in (2 * g, 2 * g + 1):
-                    landed(da, at, p).wait_recv()
-                attend(da, at, g)
-
-            return carry
-
-        lax.fori_loop(1, inner, one, 0)
 
     def give(h, to):
         return pltpu.make_async_remote_copy(
@@ -255,38 +225,93 @@
         )
 
     def finish(g):
-        for j in range(group):
+        def one(j, carry):
             h = g * group + j
             total = acc[h]
             done[h] = (total[:, :size] / total[:, size:]).astype(jnp.bfloat16)
             for step in range(1, heads):
                 give(h, (place + step) % heads).start()
-        for j in range(group):
-            h = g * group + j
             out_ref[:, pl.ds(pl.multiple_of((place * q_heads + h) * size, size), size)] = done[
                 h, pl.ds(pl.multiple_of(place * out_rows, out_rows), out_rows), :
             ]
-
-    groups = range(kv_heads)
-    for g in groups:
-        attend(0, b, g, first=True)
-    for da in range(1, reach):
-        pass_on(da, 0, 1)
-        for g in groups:
-            column_block(da, g)
-            if g + 1 < kv_heads:
-                pass_on(da, 2 * g + 2, 2 * g + 3)
-            inner_blocks(da - 1, g)
-    for g in groups:
-        pass_on(reach, 2 * g)
-        inner_blocks(reach - 1, g)
-        pass_on(reach, 2 * g + 1)
-        if g > 0:
-            inner_blocks(reach, g - 1)
-            finish(g - 1)
-        column_block(reach, g)
-    inner_blocks(reach, kv_heads - 1)
-    finish(kv_heads - 1)
+            return carry
+
+        lax.fori_loop(0, group, one, 0)
+
+    def order(first):
+        steps = [dict(g=g) for g in range(kv_heads)]
+        for da in range(1, reach):
+            for g in range(kv_heads):
+                steps.append(dict(take=3, take_da=da, take_g=g, da=da, g=g))
+                steps.append(dict(others=1, da=da - 1, g=g))
+        if first:
+            for g in range(kv_heads):
+                steps.append(dict(others=1, da=reach - 1, g=g))
+            for g in range(kv_heads):
+                steps.append(dict(take=3, take_da=reach, take_g=g, da=reach, g=g))
+                steps.append(dict(others=1, da=reach, g=g, last=1))
+        else:
+            steps.append(dict(take=3, take_da=reach, take_g=0, da=reach, g=0))
+            for g in range(kv_heads):
+                more = int(g + 1 < kv_heads)
+                steps.append(dict(take=more, take_da=reach, take_g=g + more, others=1, da=reach - 1, g=g))
+                steps.append(dict(take=2 * more, take_da=reach, take_g=g + more, others=1, da=reach, g=g, last=1))
+                if more:
+                    steps.append(dict(da=reach, g=g + 1))
+        return steps
+
+    orders = order(True), order(False)
+    step_count = len(orders[0])
+    fields = ("take", "take_da", "take_g", "others", "da", "g", "last")
+    base = 1 + max(3, reach, kv_heads)
+
+    def coded(step):
+        code = 0
+        for name in fields:
+            code = code * base + step.get(name, 0)
+        return code
+
+    def body(i, carry):
+        code = jnp.int32(0)
+        for n in range(step_count):
+            both = [coded(steps[n]) for steps in orders]
+            code = jnp.where(i == n, jnp.where(b == 0, both[0], both[1]), code)
+        now = {}
+        for name in reversed(fields):
+            now[name] = code % base
+            code = code // base
+        take, take_da, take_g = now["take"], now["take_da"], now["take_g"]
+        others, da, g = now["others"], now["da"], now["g"]
+
+        for kind in range(2):
+            @pl.when((take // (1 + kind) % 2 == 1) & (a >= take_da))
+            def _():
+                landed(take_da, b, take_g, kind).wait_recv()
+                spread(take_da, take_g, kind, lambda copy: copy.start())
+
+        def one(step, carry):
+            at = (b + step) % inner
+
+            @pl.when((a >= da) & ((step == 0) | needed(da, at, b)))
+            def _():
+                @pl.when(step > 0)
+                def _():
+                    for kind in range(2):
+                        landed(da, at, g, kind).wait_recv()
+
+                attend(da, at, g)
+
+            return carry
+
+        lax.fori_loop(others, jnp.where(others == 1, inner, 1), one, 0)
+
+        @pl.when(now["last"] == 1)
+        def _():
+            finish(g)
+
+        return carry
+
+    lax.fori_loop(0, step_count, body, 0)
 
     for h in range(q_heads):
         for step in range(1, heads):
@@ -294,8 +319,9 @@
     for da in range(reach + 1):
         @pl.when(a >= da)
         def _():
-            for p in range(pieces):
-                spread(da, p, lambda copy: copy.wait_send())
+            for g in range(kv_heads):
+                for kind in range(2):
+                    spread(da, g, kind, lambda copy: copy.wait_send())
     for h in range(q_heads):
         for step in range(1, heads):
             give(h, (place + step) % heads).wait_send()
@@ -326,7 +352,7 @@
             pltpu.VMEM((q_heads, rows, 2 * size), jnp.float32),
             pltpu.VMEM((q_heads, rows, size), jnp.bfloat16),
             pltpu.VMEM((rows, size), jnp.float32),
-            pltpu.SemaphoreType.DMA((reach, 2 * kv_heads)),
+            pltpu.SemaphoreType.DMA((reach + 1, 2 * kv_heads)),
             pltpu.SemaphoreType.DMA((reach + 1, inner, 2 * kv_heads)),
             pltpu.SemaphoreType.DMA((reach + 1, inner, 2 * kv_heads)),
             pltpu.SemaphoreType.DMA((q_heads, heads)),

time: 27 us -> 26.6 us (0.985)
  Pallas kernels: 26 us -> 25.7 us
    pallas_call x1, Pallas kernels: 26 us -> 25.7 us  [local(): pl.pallas_call(functools.partial(kernel, outer, inner, heads), out_shape=...]
where the time goes in v6:
time: 26.6 us; the launch traced here: 26.5 us
  Pallas kernels  25.7 us (97%)
  local copies, waits for them, and re-layouts  0.8 us (3%)
    pallas_call x1, Pallas kernels, local(): pl.pallas_call(functools.partial(kernel, outer, inner, heads), out_shape=...  25.7 us
    unnamed x1, local copies, waits for them, and re-layouts  0.8 us

profile of v6, /device:TPU:17, one launch (start us, length us, event | category | flops | bytes accessed | tf_op | source)
XLA Modules:
  0.0 26.5 jit_solution(12027411772809164177)
XLA Ops:
  0.0 25.7 %shard_map.46 = bf16[64,4096]{1,0:T(8,128)(2,1)S(1)} custom-call(bf16[2048,128]{1,0:T(8,128)(2,1)} %bitcast.4, bf16[512,128]{1,0:T(8,128)(2,1)} %bitcast.5, bf16[512,128]{1,0:T(8,128)(2,1)} %bitcast.6, s32[2,128]{1,0:T(2,128)} %bitcast.7), custom_call_target="tpu_custom_call" | custom-call | tf_op jit(solution)/shard_map/pallas_call | solution.py:338
  25.7 0.8 %copy.6 = bf16[64,4096]{1,0:T(8,128)(2,1)} copy(bf16[64,4096]{1,0:T(8,128)(2,1)S(1)} %shard_map.46) | data formatting | bytes 1048576

commit v7 on v4

--- a/solution.py
+++ b/solution.py
@@ -24,14 +24,14 @@
     if len(moved) != 1:
         return 1
     inner = len({place[moved[0]] for place in places})
-    return inner if count % (2 * inner) == 0 else 1
+    return inner if count % (4 * inner) == 0 else 1
 
 
 def kernel(
     outer, inner, heads,
     q_hbm, k_hbm, v_hbm, id_hbm, out_ref,
     q_ref, k_ref, v_ref, id_ref, loaded, kv, qs, top, acc, probs, done, id_col,
-    along_send, across_send, direct_send, block_recv, out_send, out_recv,
+    along_send, across_send, block_recv, out_send, out_recv,
 ):
     reach = outer // 2
     q_heads, rows, size = qs.shape
@@ -75,15 +75,6 @@
         greet({"ctx": a * inner + (b + step) % inner})
     for step in range(1, heads):
         greet({"head": (place + step) % heads})
-
-    for step in range(1, inner):
-        @pl.when(has_next & (step <= b))
-        def _():
-            greet({"ctx": me + inner - step})
-
-        @pl.when(has_prev & (b + step < inner))
-        def _():
-            greet({"ctx": me - inner + step})
 
     def split_heads(ref, count, store):
         chunk = min(256, ref.shape[0])
@@ -119,7 +110,7 @@
     kv[0, b, 0, rows:rows + ID_ROWS, :] = lines.astype(jnp.bfloat16)
 
     up, down = has_next.astype(jnp.int32), has_prev.astype(jnp.int32)
-    greeted = up * (1 + b) + down * (inner - b) + (inner - 1) + (heads - 1)
+    greeted = up + down + (inner - 1) + (heads - 1)
     pl.semaphore_wait(barrier, greeted)
 
     def along(da, p):
@@ -142,17 +133,6 @@
             device_id_type=MESH,
         )
 
-    def direct(step):
-        p = pieces - 1
-        return pltpu.make_async_remote_copy(
-            src_ref=kv.at[reach - 1, b, p, span(p)],
-            dst_ref=kv.at[reach, b, p, span(p)],
-            send_sem=direct_send.at[step],
-            recv_sem=block_recv.at[reach, b, p],
-            device_id={"ctx": me + inner - step},
-            device_id_type=MESH,
-        )
-
     def landed(da, at, p):
         return pltpu.make_async_remote_copy(
             src_ref=kv.at[da, at, p, span(p)],
@@ -177,18 +157,12 @@
                 act(along(da, p))
         for step in range(1, inner):
             to = (b + step) % inner
-            if p == pieces - 1 and da == reach - 1:
-                @pl.when(has_next & (step <= b))
-                def _():
-                    act(direct(step))
-            if p == pieces - 1 and da == reach:
-                continue
 
             @pl.when(needed(da, b, to))
             def _():
                 act(across(da, p, to))
 
-    for p in range(pieces):
+    for p in (0, 1):
         spread(0, p, lambda copy: copy.start())
 
     loads[3].wait()
@@ -338,41 +312,43 @@
     groups = range(kv_heads)
     for g in groups:
         attend(0, b, g, first=True)
-    for da in range(1, reach):
-        pass_on(da, 0, 1)
-        for g in groups:
-            column_block(da, g)
-            if g + 1 < kv_heads:
+    def enter(g):
+        pass_on(1, 2 * g, 2 * g + 1)
+        if g + 1 < kv_heads:
+            for p in (2 * g + 2, 2 * g + 3):
+                spread(0, p, lambda copy: copy.start())
+        column_block(1, g)
+
+    enter(0)
+    for g in groups:
+        inner_blocks(0, g)
+        for da in range(2, reach + 1):
+            @pl.when(b > 0)
+            def _():
+                pass_on(da, 2 * g, 2 * g + 1)
+                column_block(da, g)
+                if da < reach:
+                    inner_blocks(da - 1, g)
+
+            @pl.when(b == 0)
+            def _():
                 inner_blocks(da - 1, g)
-                pass_on(da, 2 * g + 2, 2 * g + 3)
-            else:
-                inner_blocks(da - 1, g)
-
-    @pl.when(b > 0)
-    def _():
-        pass_on(reach, 0, 1)
-        for g in groups:
-            column_block(reach, g)
-            if g + 1 < kv_heads:
-                pass_on(reach, 2 * g + 2, 2 * g + 3)
-            inner_blocks(reach, g)
-            if reach > 1 and inner > 1:
+                pass_on(da, 2 * g, 2 * g + 1)
+                column_block(da, g)
+
+        if g + 1 < kv_heads:
+            enter(g + 1)
+        if inner > 1:
+            @pl.when(b > 0)
+            def _():
+                inner_blocks(reach, g)
                 inner_blocks(reach - 1, g, last=True)
-            else:
-                inner_blocks(reach - 1, g)
-                finish(g)
-
-    @pl.when(b == 0)
-    def _():
-        for g in groups:
-            inner_blocks(reach - 1, g)
-        for g in groups:
-            pass_on(reach, 2 * g, 2 * g + 1)
-            column_block(reach, g)
-            if inner > 1:
+
+            @pl.when(b == 0)
+            def _():
                 inner_blocks(reach, g, last=True)
-            else:
-                finish(g)
+        else:
+            finish(g)
 
     for h in range(q_heads):
         for step in range(1, heads):
@@ -415,7 +391,6 @@
             pltpu.VMEM((rows, size), jnp.float32),
             pltpu.SemaphoreType.DMA((reach, 2 * kv_heads)),
             pltpu.SemaphoreType.DMA((reach + 1, inner, 2 * kv_heads)),
-            pltpu.SemaphoreType.DMA((inner,)),
             pltpu.SemaphoreType.DMA((reach + 1, inner, 2 * kv_heads)),
             pltpu.SemaphoreType.DMA((q_heads, heads)),
             pltpu.SemaphoreType.DMA((q_heads, heads)),

time: 26.3 us -> 26.5 us (level)
  no operation moved by 1% of the time
where the time goes in v7:
time: 26.5 us; the launch traced here: 26.3 us
  Pallas kernels  25.5 us (96%)
  local copies, waits for them, and re-layouts  0.8 us (3%)
    pallas_call x1, Pallas kernels, local(): pl.pallas_call(functools.partial(kernel, outer, inner, heads), out_shape=...  25.5 us
    unnamed x1, local copies, waits for them, and re-layouts  0.8 us

profile of v7, /device:TPU:17, one launch (start us, length us, event | category | flops | bytes accessed | tf_op | source)
XLA Modules:
  0.0 26.3 jit_solution(17304606127273073139)
XLA Ops:
  0.0 25.5 %shard_map.46 = bf16[64,4096]{1,0:T(8,128)(2,1)S(1)} custom-call(bf16[2048,128]{1,0:T(8,128)(2,1)} %bitcast.4, bf16[512,128]{1,0:T(8,128)(2,1)} %bitcast.5, bf16[512,128]{1,0:T(8,128)(2,1)} %bitcast.6, s32[2,128]{1,0:T(2,128)} %bitcast.7), custom_call_target="tpu_custom_call" | custom-call | tf_op jit(solution)/shard_map/pallas_call | solution.py:374
  25.5 0.8 %copy.6 = bf16[64,4096]{1,0:T(8,128)(2,1)} copy(bf16[64,4096]{1,0:T(8,128)(2,1)S(1)} %shard_map.46) | data formatting | bytes 1048576

commit v8 on v7

--- a/solution.py
+++ b/solution.py
@@ -162,7 +162,7 @@
             def _():
                 act(across(da, p, to))
 
-    for p in (0, 1):
+    for p in range(pieces):
         spread(0, p, lambda copy: copy.start())
 
     loads[3].wait()
@@ -314,9 +314,6 @@
         attend(0, b, g, first=True)
     def enter(g):
         pass_on(1, 2 * g, 2 * g + 1)
-        if g + 1 < kv_heads:
-            for p in (2 * g + 2, 2 * g + 3):
-                spread(0, p, lambda copy: copy.start())
         column_block(1, g)
 
     enter(0)

time: 26.5 us -> 27.5 us (1.038)
  Pallas kernels: 25.5 us -> 26.5 us
    pallas_call x1, Pallas kernels: 25.5 us -> 26.5 us  [local(): pl.pallas_call(functools.partial(kernel, outer, inner, heads), out_shape=...]
where the time goes in v8:
time: 27.5 us; the launch traced here: 27.3 us
  Pallas kernels  26.5 us (96%)
  local copies, waits for them, and re-layouts  0.8 us (3%)
    pallas_call x1, Pallas kernels, local(): pl.pallas_call(functools.partial(kernel, outer, inner, heads), out_shape=...  26.5 us
    unnamed x1, local copies, waits for them, and re-layouts  0.8 us

profile of v8, /device:TPU:17, one launch (start us, length us, event | category | flops | bytes accessed | tf_op | source)
XLA Modules:
  0.0 27.3 jit_solution(4580680296085479752)
XLA Ops:
  0.0 26.5 %shard_map.46 = bf16[64,4096]{1,0:T(8,128)(2,1)S(1)} custom-call(bf16[2048,128]{1,0:T(8,128)(2,1)} %bitcast.4, bf16[512,128]{1,0:T(8,128)(2,1)} %bitcast.5, bf16[512,128]{1,0:T(8,128)(2,1)} %bitcast.6, s32[2,128]{1,0:T(2,128)} %bitcast.7), custom_call_target="tpu_custom_call" | custom-call | tf_op jit(solution)/shard_map/pallas_call | solution.py:371
  26.5 0.8 %copy.6 = bf16[64,4096]{1,0:T(8,128)(2,1)} copy(bf16[64,4096]{1,0:T(8,128)(2,1)S(1)} %shard_map.46) | data formatting | bytes 1048576
